TPU v7x, 256 devices: a whole 4x4x8 slice. The times are simulated.
256 devices in a mesh: row: 16 (over z, core), col: 8 (over y_hi, x), rep: 2 (over y_lo).
Axes of the slice: x: 4, y: 4 (y_hi: 2, y_lo: 2; y = y_hi * 2 + y_lo), z: 8, core: 2. Of those that a mesh axis runs over, the one named last changes fastest.
Arguments:
- node_features: bfloat16 [65536, 256], P(('row', 'col', 'rep')), may hold values from -6 to 6
- weight: bfloat16 [256, 256], replicated, may hold values from -0.375 to 0.375
- cotangent: bfloat16 [65536, 256], P(('col', 'rep', 'row')), may hold values from -6 to 6
- adjacency_blocks: bfloat16 [16, 16, 256, 128, 128], P(('col', 'rep'), 'row'), may hold values from -0.0625 to 0.0625
- block_coords: int32 [16, 16, 2, 256], P(('col', 'rep'), 'row'), may hold values from 0 to 31, as said below
- block_counts: int32 [16, 16], P(('col', 'rep'), 'row'), may hold values from 1 to 256, as said below
Outputs:
- hidden: bfloat16 [65536, 256], P(('col', 'rep', 'row'))
- weight_grad: float32 [256, 256], replicated
- feature_grad: bfloat16 [65536, 256], P(('row', 'col', 'rep'))
Inputs may be any that keep to these rules, and one draw needn't show every extreme that they name: block_coords[i, r, 0, k] is a block row below 32 and block_coords[i, r, 1, k] a block column below 32; within a tile the first min(256, 1024) slots name distinct positions. Only the first block_counts[i, r] slots of tile (i, r) belong to the adjacency; the values and coordinates in its other slots are not part of it.
All inputs are finite; a program needn't handle non-finite values.
Results may differ from a plain program's by a relative error of at most 0.029.
Values may be sent and summed in bfloat16 or wider, within the bound.
No kernel may reach another device: no remote copies, remote signals or barrier semaphores. Data moves between devices by JAX's collectives and lax.ppermute only.
A program may use at most 128 MiB of HBM per device.

v0:
```python
import math
import jax
import jax.numpy as jnp
from jax import lax
from jax.sharding import PartitionSpec as P


def silu_slope(values):
    sigma = jax.nn.sigmoid(values)
    return sigma * (1.0 + values * (1.0 - sigma))


def tile_product(blocks, coords, filled, source, out_blocks, flipped):
    slot_total = blocks.shape[0]
    block_size = blocks.shape[1]
    feature_width = source.shape[1]
    group_size = math.gcd(slot_total, 64)
    groups = slot_total // group_size
    source_blocks = source.reshape(-1, block_size, feature_width)
    take_index = coords[0] if flipped else coords[1]
    put_index = coords[1] if flipped else coords[0]
    active = (jnp.arange(slot_total, dtype=jnp.int32) < filled).astype(jnp.float32)
    einsum_form = "kba,kbf->kaf" if flipped else "kab,kbf->kaf"
    targets = jnp.arange(out_blocks, dtype=jnp.int32)

    def accumulate(running, pieces):
        block_group, take_group, put_group, active_group = pieces
        gathered = source_blocks[take_group]
        product = jnp.einsum(einsum_form, block_group, gathered, preferred_element_type=jnp.float32)
        placing = (put_group[:, None] == targets[None, :]).astype(jnp.float32) * active_group[
            :, None
        ]
        flat = product.reshape(group_size, block_size * feature_width)
        placed = lax.dot_general(
            placing,
            flat,
            (((0,), (0,)), ((), ())),
            precision=lax.Precision.HIGHEST,
            preferred_element_type=jnp.float32,
        )
        return (running + placed, None)

    running = jnp.zeros((out_blocks, block_size * feature_width), jnp.float32)
    running, _ = lax.scan(
        accumulate,
        running,
        (
            blocks.reshape(groups, group_size, block_size, block_size),
            take_index.reshape(groups, group_size),
            put_index.reshape(groups, group_size),
            active.reshape(groups, group_size),
        ),
    )
    return running.reshape(out_blocks * block_size, feature_width)


def body(node_features, weight, cotangent, adjacency_blocks, block_coords, block_counts):
    blocks = adjacency_blocks[0, 0]
    coords = block_coords[0, 0]
    filled = block_counts[0, 0]
    block_size = blocks.shape[-1]
    local_nodes = node_features.shape[0]
    row_devices = lax.axis_size("row")
    node_total = local_nodes * row_devices * lax.axis_size("col") * lax.axis_size("rep")
    tile_rows = local_nodes * row_devices
    column_feats = lax.all_gather(node_features, ("col", "rep"), axis=0, tiled=True)
    tile_cols = column_feats.shape[0]
    partial_value = tile_product(
        blocks, coords, filled, column_feats, tile_rows // block_size, False
    )
    own_sum = lax.psum_scatter(
        partial_value.astype(jnp.bfloat16), "row", scatter_dimension=0, tiled=True
    )
    pre_act = jnp.dot(own_sum, weight, preferred_element_type=jnp.float32)
    hidden = jax.nn.silu(pre_act).astype(jnp.bfloat16)
    own_grad = (cotangent.astype(jnp.float32) * silu_slope(pre_act)).astype(jnp.bfloat16)
    own_mixed_grad = jnp.dot(own_grad, weight.T, preferred_element_type=jnp.float32).astype(
        jnp.bfloat16
    )
    panel_grad = lax.all_gather(own_mixed_grad, "row", axis=0, tiled=True)
    weight_part = lax.dot_general(
        own_sum, own_grad, (((0,), (0,)), ((), ())), preferred_element_type=jnp.float32
    )
    weight_grad = lax.psum(weight_part, ("row", "col", "rep")) / math.sqrt(node_total)
    back_terms = tile_product(blocks, coords, filled, panel_grad, tile_cols // block_size, True)
    feature_grad = lax.psum_scatter(
        back_terms.astype(jnp.bfloat16), ("col", "rep"), scatter_dimension=0, tiled=True
    )
    return (hidden, weight_grad, feature_grad)


def solution(mesh):
    in_specs = (
        P(("row", "col", "rep"), None),
        P(),
        P(("col", "rep", "row"), None),
        P(("col", "rep"), "row", None, None, None),
        P(("col", "rep"), "row", None, None),
        P(("col", "rep"), "row"),
    )
    out_specs = (P(("col", "rep", "row"), None), P(), P(("row", "col", "rep"), None))
    return jax.shard_map(body, mesh=mesh, in_specs=in_specs, out_specs=out_specs, check_vma=False)
```

profile of v0, /device:TPU:32, one launch (start us, length us, event | category | flops | bytes accessed | tf_op | source)
XLA Modules:
  0.0 642.4 jit_solution(17018396184696318942)
XLA Ops:
  9.6 81.7 %all-gather.3.cloned.1.call-done = bf16[4096,256]{1,0:T(8,128)(2,1)} async-done(((bf16[256,256]{1,0:T(8,128)(2,1)}), bf16[4096,256]{1,0:T(8,128)(2,1)}) %all-gather.3.cloned.1.call-update) | async-done | bytes 2097168 | tf_op jit(solution)/shard_map/all_gather | solution.py:66
  91.3 99.7 %while.22 = (s32[]{:T(128)}, f32[32,32768]{1,0:T(8,128)}, s32[4,64]{1,0:T(4,128)S(1)}, f32[4,64]{1,0:T(4,128)S(1)}, bf16[4,64,128,128]{3,2,1,0:T(8,128)(2,1)}, /...) while((s32[]{:T(128)}, f32[32,32768]{1,0:T(8,128)}, ...), condition=%wide.region_1.2_spmd.clone, body=%wide.region_0.1_spmd.clone.sunk | while | flops 1344279808 | bytes 56630384 | solution.py:44
  91.3 4.3 gather_fusion
  95.7 4.1 fusion.63
  99.7 8.0 %copy.16 = f32[8,8,128,256]{3,1,2,0:T(8,128)} copy(f32[8,8,128,256]{3,2,1,0:T(8,128)S(1)} %bitcast.88) | data formatting | bytes 16777216 | tf_op jit(solution)/shard_map/while
  107.7 8.0 %convolution_add_fusion.4 = f32[32,32768]{1,0:T(8,128)} fusion(f32[64,32768]{1,0:T(8,128)} %bitcast.86, f32[32,32768]{1,0:T(8,128)} %get-tuple-element.276, pred[]{:T(512)S(6)} %compare.6, f32[64]{0:T(128)S(1)} %fusion.64, s32[64]{0:T(128)S(1)} %fusion.65), kind=kOutput, calls=%fused_computation.4.clone.1 | convolution fusion | flops 807407616 | bytes 16777728 | tf_op jit(solution)/shard_map/while/body/eval_jaxpr/dot_general | solution.py:34
  115.7 4.3 gather_fusion
  120.1 4.1 fusion.63
  124.1 8.0 %copy.16 = f32[8,8,128,256]{3,1,2,0:T(8,128)} copy(f32[8,8,128,256]{3,2,1,0:T(8,128)S(1)} %bitcast.88) | data formatting | bytes 16777216 | tf_op jit(solution)/shard_map/while
  132.1 8.7 %convolution_add_fusion.4 = f32[32,32768]{1,0:T(8,128)} fusion(f32[64,32768]{1,0:T(8,128)} %bitcast.86, f32[32,32768]{1,0:T(8,128)} %get-tuple-element.276, pred[]{:T(512)S(6)} %compare.6, f32[64]{0:T(128)S(1)} %fusion.64, s32[64]{0:T(128)S(1)} %fusion.65), kind=kOutput, calls=%fused_computation.4.clone.1 | convolution fusion | flops 807407616 | bytes 16777728 | tf_op jit(solution)/shard_map/while/body/eval_jaxpr/dot_general | solution.py:34
  140.8 4.3 gather_fusion
  145.2 4.1 fusion.63
  149.2 8.0 %copy.16 = f32[8,8,128,256]{3,1,2,0:T(8,128)} copy(f32[8,8,128,256]{3,2,1,0:T(8,128)S(1)} %bitcast.88) | data formatting | bytes 16777216 | tf_op jit(solution)/shard_map/while
  157.2 8.7 %convolution_add_fusion.4 = f32[32,32768]{1,0:T(8,128)} fusion(f32[64,32768]{1,0:T(8,128)} %bitcast.86, f32[32,32768]{1,0:T(8,128)} %get-tuple-element.276, pred[]{:T(512)S(6)} %compare.6, f32[64]{0:T(128)S(1)} %fusion.64, s32[64]{0:T(128)S(1)} %fusion.65), kind=kOutput, calls=%fused_computation.4.clone.1 | convolution fusion | flops 807407616 | bytes 16777728 | tf_op jit(solution)/shard_map/while/body/eval_jaxpr/dot_general | solution.py:34
  165.9 4.3 gather_fusion
  170.2 4.1 fusion.63
  174.3 8.0 %copy.16 = f32[8,8,128,256]{3,1,2,0:T(8,128)} copy(f32[8,8,128,256]{3,2,1,0:T(8,128)S(1)} %bitcast.88) | data formatting | bytes 16777216 | tf_op jit(solution)/shard_map/while
  182.3 8.7 %convolution_add_fusion.4 = f32[32,32768]{1,0:T(8,128)} fusion(f32[64,32768]{1,0:T(8,128)} %bitcast.86, f32[32,32768]{1,0:T(8,128)} %get-tuple-element.276, pred[]{:T(512)S(6)} %compare.6, f32[64]{0:T(128)S(1)} %fusion.64, s32[64]{0:T(128)S(1)} %fusion.65), kind=kOutput, calls=%fused_computation.4.clone.1 | convolution fusion | flops 807407616 | bytes 16777728 | tf_op jit(solution)/shard_map/while/body/eval_jaxpr/dot_general | solution.py:34
  191.0 2.4 convert_element_type.32
  193.4 2.4 convert_element_type.33
  195.8 56.5 %reduce-scatter.3.cloned.1.call-done = bf16[256,256]{1,0:T(8,128)(2,1)} async-done(((bf16[4096,256]{1,0:T(8,128)(2,1)}), bf16[256,256]{1,0:T(8,128)(2,1)}) %reduce-scatter.3.cloned.1.call-update) | async-done | bytes 131088 | tf_op jit(solution)/shard_map/reduce_scatter | solution.py:71
  252.3 1.8 multiply_convert_fusion
  254.1 0.9 convolution_convert_fusion
  255.1 12.0 %copy.9 = bf16[1,1,256,128,128]{3,4,2,1,0:T(8,128)(2,1)} copy(bf16[1,1,256,128,128]{4,3,2,1,0:T(8,128)(2,1)} %bitcast.93) | data formatting | bytes 16777216 | tf_op args[3]
  267.1 0.9 fusion.31
  268.3 27.7 %all-gather.5.cloned.1.call-done = bf16[4096,256]{1,0:T(8,128)(2,1)} async-done(((bf16[256,256]{1,0:T(8,128)(2,1)}), bf16[4096,256]{1,0:T(8,128)(2,1)}) %all-gather.5.cloned.1.call-update) | async-done | bytes 2097168 | tf_op jit(solution)/shard_map/all_gather | solution.py:80
  296.0 99.8 %while.23 = (s32[]{:T(128)}, f32[32,32768]{1,0:T(8,128)}, s32[4,64]{1,0:T(4,128)S(1)}, f32[4,64]{1,0:T(4,128)S(1)}, bf16[4,64,128,128]{2,3,1,0:T(8,128)(2,1)}, /...) while((s32[]{:T(128)}, f32[32,32768]{1,0:T(8,128)}, ...), condition=%wide.region_5.6_spmd.clone, body=%wide.region_4.5_spmd.clone.sunk | while | flops 1344279808 | bytes 56630384 | solution.py:44
  296.0 4.4 gather_fusion.1
  300.4 4.1 fusion.71
  304.5 8.0 %copy.17 = f32[8,8,128,256]{3,1,2,0:T(8,128)} copy(f32[8,8,128,256]{3,2,1,0:T(8,128)S(1)} %bitcast.89) | data formatting | bytes 16777216 | tf_op jit(solution)/shard_map/while
  312.4 8.0 %convolution_add_fusion.5 = f32[32,32768]{1,0:T(8,128)} fusion(f32[64,32768]{1,0:T(8,128)} %bitcast.87, f32[32,32768]{1,0:T(8,128)} %get-tuple-element.303, pred[]{:T(512)S(6)} %compare.7, f32[64]{0:T(128)S(1)} %fusion.72, s32[64]{0:T(128)S(1)} %fusion.73), kind=kOutput, calls=%fused_computation.24.clone.1 | convolution fusion | flops 807407616 | bytes 16777728 | tf_op jit(solution)/shard_map/while/body/eval_jaxpr/dot_general | solution.py:34
  320.4 4.4 gather_fusion.1
  324.8 4.1 fusion.71
  328.9 8.0 %copy.17 = f32[8,8,128,256]{3,1,2,0:T(8,128)} copy(f32[8,8,128,256]{3,2,1,0:T(8,128)S(1)} %bitcast.89) | data formatting | bytes 16777216 | tf_op jit(solution)/shard_map/while
  336.9 8.7 %convolution_add_fusion.5 = f32[32,32768]{1,0:T(8,128)} fusion(f32[64,32768]{1,0:T(8,128)} %bitcast.87, f32[32,32768]{1,0:T(8,128)} %get-tuple-element.303, pred[]{:T(512)S(6)} %compare.7, f32[64]{0:T(128)S(1)} %fusion.72, s32[64]{0:T(128)S(1)} %fusion.73), kind=kOutput, calls=%fused_computation.24.clone.1 | convolution fusion | flops 807407616 | bytes 16777728 | tf_op jit(solution)/shard_map/while/body/eval_jaxpr/dot_general | solution.py:34
  345.6 4.4 gather_fusion.1
  350.0 4.1 fusion.71
  354.1 8.0 %copy.17 = f32[8,8,128,256]{3,1,2,0:T(8,128)} copy(f32[8,8,128,256]{3,2,1,0:T(8,128)S(1)} %bitcast.89) | data formatting | bytes 16777216 | tf_op jit(solution)/shard_map/while
  362.0 8.6 %convolution_add_fusion.5 = f32[32,32768]{1,0:T(8,128)} fusion(f32[64,32768]{1,0:T(8,128)} %bitcast.87, f32[32,32768]{1,0:T(8,128)} %get-tuple-element.303, pred[]{:T(512)S(6)} %compare.7, f32[64]{0:T(128)S(1)} %fusion.72, s32[64]{0:T(128)S(1)} %fusion.73), kind=kOutput, calls=%fused_computation.24.clone.1 | convolution fusion | flops 807407616 | bytes 16777728 | tf_op jit(solution)/shard_map/while/body/eval_jaxpr/dot_general | solution.py:34
  370.7 4.4 gather_fusion.1
  375.1 4.1 fusion.71
  379.2 8.0 %copy.17 = f32[8,8,128,256]{3,1,2,0:T(8,128)} copy(f32[8,8,128,256]{3,2,1,0:T(8,128)S(1)} %bitcast.89) | data formatting | bytes 16777216 | tf_op jit(solution)/shard_map/while
  387.1 8.7 %convolution_add_fusion.5 = f32[32,32768]{1,0:T(8,128)} fusion(f32[64,32768]{1,0:T(8,128)} %bitcast.87, f32[32,32768]{1,0:T(8,128)} %get-tuple-element.303, pred[]{:T(512)S(6)} %compare.7, f32[64]{0:T(128)S(1)} %fusion.72, s32[64]{0:T(128)S(1)} %fusion.73), kind=kOutput, calls=%fused_computation.24.clone.1 | convolution fusion | flops 807407616 | bytes 16777728 | tf_op jit(solution)/shard_map/while/body/eval_jaxpr/dot_general | solution.py:34
  395.8 2.4 convert_element_type.38
  398.2 2.4 convert_element_type.39
  400.6 148.2 %all-reduce.2.cloned.1.call-done = f32[256,256]{1,0:T(8,128)} async-done(((f32[256,256]{1,0:T(8,128)}), f32[256,256]{1,0:T(8,128)}) %all-reduce.2.cloned.1.call-update) | async-done | bytes 262160 | tf_op jit(solution)/shard_map/psum | solution.py:84
  548.9 1.7 broadcast_multiply_fusion
  550.5 85.3 %reduce-scatter.5.cloned.1.call-done = bf16[256,256]{1,0:T(8,128)(2,1)} async-done(((bf16[4096,256]{1,0:T(8,128)(2,1)}), bf16[256,256]{1,0:T(8,128)(2,1)}) %reduce-scatter.5.cloned.1.call-update) | async-done | bytes 131088 | tf_op jit(solution)/shard_map/reduce_scatter | solution.py:86
  (56 shorter events, 2.3 us)
Async XLA Ops:
  7.2 245.1 %copy-start = (bf16[256,256]{1,0:T(8,128)(2,1)S(1)}, bf16[256,256]{1,0:T(8,128)(2,1)}, u32[]{:S(2)}) copy-start(bf16[256,256]{1,0:T(8,128)(2,1)} %param.11) | copy-start | bytes 393220
  7.2 84.1 %all-gather.3.cloned.1.call-start = ((), (), s32[]{:S(2)}) async-start(), calls=%async_computation.2 | async-start | bytes 2228224 | tf_op jit(solution)/shard_map/all_gather | solution.py:66
  7.9 244.4 %reduce-scatter.3.cloned.1.call-start = ((), (), s32[]{:S(2)}) async-start(), calls=%async_computation.3 | async-start | bytes 2228224 | tf_op jit(solution)/shard_map/reduce_scatter | solution.py:71
  193.4 58.9 %copy-start.3 = (bf16[256,256]{1,0:T(8,128)(2,1)S(1)}, bf16[256,256]{1,0:T(8,128)(2,1)}, u32[]{:S(2)}) copy-start(bf16[256,256]{1,0:T(8,128)(2,1)} %param.12) | copy-start | bytes 393220
  195.8 100.3 %all-gather.5.cloned.1.call-start = ((), (), s32[]{:S(2)}) async-start(), calls=%async_computation.5 | async-start | bytes 2228224 | tf_op jit(solution)/shard_map/all_gather | solution.py:80
  255.0 12.1 %copy-start.2 = (bf16[256,256]{1,0:T(8,128)(2,1)S(1)}, bf16[256,256]{1,0:T(8,128)(2,1)}, u32[]{:S(2)}) copy-start(bf16[256,256]{1,0:T(8,128)(2,1)} %reduce-scatter.3.cloned.1.call-done) | copy-start | bytes 393220
  255.0 293.8 %all-reduce.2.cloned.1.call-start = ((), (), s32[]{:S(2)}) async-start(), calls=%async_computation.4 | async-start | bytes 524288 | tf_op jit(solution)/shard_map/psum | solution.py:84
  268.1 367.8 %reduce-scatter.5.cloned.1.call-start = ((), (), s32[]{:S(2)}) async-start(), calls=%async_computation.6 | async-start | bytes 2228224 | tf_op jit(solution)/shard_map/reduce_scatter | solution.py:86
  395.8 240.0 %copy-start.1 = (bf16[256,256]{1,0:T(8,128)(2,1)S(1)}, bf16[256,256]{1,0:T(8,128)(2,1)}, u32[]{:S(2)}) copy-start(bf16[256,256]{1,0:T(8,128)(2,1)} %param.11) | copy-start | bytes 393220
Sparse Core Ops, SparseCore 0:
  9.8 81.4 all-gather.2
  195.9 56.3 reduce-scatter.2
  255.2 40.8 all-gather.4
  301.9 246.9 all-reduce.1
  551.8 83.9 reduce-scatter.4
where the time goes:
time: 643 us; the launch traced here: 642 us
  waiting for transfers between devices  400 us (62%)
  local copies, waits for them, and re-layouts  116 us (18%)
  matrix products  104 us (16%)
  between operations  14.5 us (2%)
  other arithmetic  6.61 us (1%)
    psum x1, waiting for transfers between devices, body(): lax.psum(weight_part, ('row', 'col', 'rep')) / math.sqrt(node_total)  148 us
    reduce_scatter x1, waiting for transfers between devices, body(): lax.psum_scatter(back_terms.astype(jnp.bfloat16), ('col', 'rep'), scatter...  85.3 us
    all_gather x1, waiting for transfers between devices, body(): lax.all_gather(node_features, ('col', 'rep'), axis=0, tiled=True)  81.7 us
    dot_general x8, matrix products, accumulate(): lax.dot_general(placing, flat, (((0,), (0,)), ((), ())), precision=lax.Pr...  68 us
    while x8, local copies, waits for them, and re-layouts  63.7 us
    reduce_scatter x1, waiting for transfers between devices, body(): lax.psum_scatter(partial_value.astype(jnp.bfloat16), 'row', scatter_dimen...  56.5 us
    gather x8, local copies, waits for them, and re-layouts, accumulate(): gathered = source_blocks[take_group]  34.8 us
    dot_general x8, matrix products, accumulate(): jnp.einsum(einsum_form, block_group, gathered, preferred_element_type=jnp...  32.6 us
  transfers between devices with their start and end apart: 5, of which 5 were waited for; matrix products, arithmetic and copies ran while one was open for 19% of the time, Pallas kernels for 0%

commit v1 on v0

--- a/solution.py
+++ b/solution.py
@@ -3,6 +3,7 @@
 import jax.numpy as jnp
 from jax import lax
 from jax.sharding import PartitionSpec as P
+from jax.lax import all_to_all, axis_size
 
 
 def silu_slope(values):
@@ -63,7 +64,15 @@
     row_devices = lax.axis_size("row")
     node_total = local_nodes * row_devices * lax.axis_size("col") * lax.axis_size("rep")
     tile_rows = local_nodes * row_devices
-    column_feats = lax.all_gather(node_features, ("col", "rep"), axis=0, tiled=True)
+    column_feats = jnp.concatenate(
+        all_to_all(
+            jnp.stack(tuple((node_features for _ in range(axis_size(("col", "rep")))))),
+            axis_name=("col", "rep"),
+            split_axis=0,
+            concat_axis=0,
+        ),
+        0,
+    )
     tile_cols = column_feats.shape[0]
     partial_value = tile_product(
         blocks, coords, filled, column_feats, tile_rows // block_size, False

time: 643 us -> 591 us (0.919)
  waiting for transfers between devices: 400 us -> 346 us
  starting transfers between devices: 0.38 us -> 7.38 us
    all_gather x1 -> x0, waiting for transfers between devices: 81.7 us -> none  [body(): lax.all_gather(node_features, ('col', 'rep'), axis=0, tiled=True)]
    all_to_all x0 -> x1, waiting for transfers between devices: none -> 30.2 us  [body(): all_to_all(jnp.stack(tuple((node_features for _ in range(axis_size(('col'...]
    all_to_all x0 -> x1, starting transfers between devices: none -> 7.03 us  [body(): all_to_all(jnp.stack(tuple((node_features for _ in range(axis_size(('col'...]
  transfers between devices with their start and end apart: 5 -> 5, of which waited for: 5 -> 5; matrix products, arithmetic and copies ran while one was open for 19% -> 20% of each run, Pallas kernels for 0% -> 0%
where the time goes in v1:
time: 591 us
  waiting for transfers between devices  346 us (59%)
  local copies, waits for them, and re-layouts  112 us (19%)
  matrix products  104 us (18%)
  between operations  14.5 us (2%)
  starting transfers between devices  7.38 us (1%)
  other arithmetic  6.61 us (1%)
    psum x1, waiting for transfers between devices, body(): lax.psum(weight_part, ('row', 'col', 'rep')) / math.sqrt(node_total)  149 us
    reduce_scatter x1, waiting for transfers between devices, body(): lax.psum_scatter(back_terms.astype(jnp.bfloat16), ('col', 'rep'), scatter...  85.3 us
    dot_general x8, matrix products, accumulate(): lax.dot_general(placing, flat, (((0,), (0,)), ((), ())), precision=lax.Pr...  68 us
    while x8, local copies, waits for them, and re-layouts  63.7 us
    reduce_scatter x1, waiting for transfers between devices, body(): lax.psum_scatter(partial_value.astype(jnp.bfloat16), 'row', scatter_dimen...  54.4 us
    dot_general x8, matrix products, accumulate(): jnp.einsum(einsum_form, block_group, gathered, preferred_element_type=jnp...  32.5 us
    all_to_all x1, waiting for transfers between devices, body(): all_to_all(jnp.stack(tuple((node_features for _ in range(axis_size(('col'...  30.2 us
    gather x8, local copies, waits for them, and re-layouts, accumulate(): gathered = source_blocks[take_group]  28.5 us
  transfers between devices with their start and end apart: 5, of which 5 were waited for; matrix products, arithmetic and copies ran while one was open for 20% of the time, Pallas kernels for 0%

profile of v1, /device:TPU:32, one launch (start us, length us, event | category | flops | bytes accessed | tf_op | source)
XLA Modules:
  0.0 590.6 jit_solution(1414005611268056460)
XLA Ops:
  7.2 2.5 stack.2
  9.7 7.0 %all-to-all-start = ((bf16[16,256,256]{2,1,0:T(8,128)(2,1)}), bf16[16,256,256]{2,1,0:T(8,128)(2,1)S(1)}, u32[]{:S(2)}, u32[]{:S(2)}) async-start(bf16[16,256,256]{2,1,0:T(8,128)(2,1)} %stack.2), calls=%async_computation | async-start | bytes 4194304 | tf_op jit(solution)/shard_map/all_to_all | solution.py:68
  17.6 30.2 %all-to-all-done = bf16[16,256,256]{2,1,0:T(8,128)(2,1)S(1)} async-done(((bf16[16,256,256]{2,1,0:T(8,128)(2,1)}), bf16[16,256,256]{2,1,0:T(8,128)(2,1)S(1)}, u32[]{:S(2)}, u32[]{:S(2)}) %all-to-all-start) | async-done | bytes 2097184 | tf_op jit(solution)/shard_map/all_to_all | solution.py:68
  47.9 93.3 %while.22 = (s32[]{:T(128)}, f32[32,32768]{1,0:T(8,128)}, s32[4,64]{1,0:T(4,128)S(1)}, f32[4,64]{1,0:T(4,128)S(1)}, bf16[4,64,128,128]{3,2,1,0:T(8,128)(2,1)}, /...) while((s32[]{:T(128)}, f32[32,32768]{1,0:T(8,128)}, ...), condition=%wide.region_1.2_spmd.clone, body=%wide.region_0.1_spmd.clone.sunk | while | flops 1344279808 | bytes 56630384 | solution.py:45
  47.9 2.8 gather_fusion
  50.6 4.1 fusion.63
  54.7 8.0 %copy.16 = f32[8,8,128,256]{3,1,2,0:T(8,128)} copy(f32[8,8,128,256]{3,2,1,0:T(8,128)S(1)} %bitcast.88) | data formatting | bytes 16777216 | tf_op jit(solution)/shard_map/while
  62.7 8.0 %convolution_add_fusion.4 = f32[32,32768]{1,0:T(8,128)} fusion(f32[64,32768]{1,0:T(8,128)} %bitcast.86, f32[32,32768]{1,0:T(8,128)} %get-tuple-element.276, pred[]{:T(512)S(6)} %compare.6, f32[64]{0:T(128)S(1)} %fusion.64, s32[64]{0:T(128)S(1)} %fusion.65), kind=kOutput, calls=%fused_computation.4.clone.1 | convolution fusion | flops 807407616 | bytes 16777728 | tf_op jit(solution)/shard_map/while/body/eval_jaxpr/dot_general | solution.py:35
  70.7 2.8 gather_fusion
  73.5 4.1 fusion.63
  77.5 8.0 %copy.16 = f32[8,8,128,256]{3,1,2,0:T(8,128)} copy(f32[8,8,128,256]{3,2,1,0:T(8,128)S(1)} %bitcast.88) | data formatting | bytes 16777216 | tf_op jit(solution)/shard_map/while
  85.5 8.7 %convolution_add_fusion.4 = f32[32,32768]{1,0:T(8,128)} fusion(f32[64,32768]{1,0:T(8,128)} %bitcast.86, f32[32,32768]{1,0:T(8,128)} %get-tuple-element.276, pred[]{:T(512)S(6)} %compare.6, f32[64]{0:T(128)S(1)} %fusion.64, s32[64]{0:T(128)S(1)} %fusion.65), kind=kOutput, calls=%fused_computation.4.clone.1 | convolution fusion | flops 807407616 | bytes 16777728 | tf_op jit(solution)/shard_map/while/body/eval_jaxpr/dot_general | solution.py:35
  94.2 2.8 gather_fusion
  97.0 4.1 fusion.63
  101.0 8.0 %copy.16 = f32[8,8,128,256]{3,1,2,0:T(8,128)} copy(f32[8,8,128,256]{3,2,1,0:T(8,128)S(1)} %bitcast.88) | data formatting | bytes 16777216 | tf_op jit(solution)/shard_map/while
  109.0 8.7 %convolution_add_fusion.4 = f32[32,32768]{1,0:T(8,128)} fusion(f32[64,32768]{1,0:T(8,128)} %bitcast.86, f32[32,32768]{1,0:T(8,128)} %get-tuple-element.276, pred[]{:T(512)S(6)} %compare.6, f32[64]{0:T(128)S(1)} %fusion.64, s32[64]{0:T(128)S(1)} %fusion.65), kind=kOutput, calls=%fused_computation.4.clone.1 | convolution fusion | flops 807407616 | bytes 16777728 | tf_op jit(solution)/shard_map/while/body/eval_jaxpr/dot_general | solution.py:35
  117.7 2.8 gather_fusion
  120.4 4.1 fusion.63
  124.5 8.0 %copy.16 = f32[8,8,128,256]{3,1,2,0:T(8,128)} copy(f32[8,8,128,256]{3,2,1,0:T(8,128)S(1)} %bitcast.88) | data formatting | bytes 16777216 | tf_op jit(solution)/shard_map/while
  132.5 8.7 %convolution_add_fusion.4 = f32[32,32768]{1,0:T(8,128)} fusion(f32[64,32768]{1,0:T(8,128)} %bitcast.86, f32[32,32768]{1,0:T(8,128)} %get-tuple-element.276, pred[]{:T(512)S(6)} %compare.6, f32[64]{0:T(128)S(1)} %fusion.64, s32[64]{0:T(128)S(1)} %fusion.65), kind=kOutput, calls=%fused_computation.4.clone.1 | convolution fusion | flops 807407616 | bytes 16777728 | tf_op jit(solution)/shard_map/while/body/eval_jaxpr/dot_general | solution.py:35
  141.2 2.4 convert_element_type.32
  143.6 2.4 convert_element_type.33
  146.0 54.4 %reduce-scatter.3.cloned.1.call-done = bf16[256,256]{1,0:T(8,128)(2,1)} async-done(((bf16[4096,256]{1,0:T(8,128)(2,1)}), bf16[256,256]{1,0:T(8,128)(2,1)}) %reduce-scatter.3.cloned.1.call-update) | async-done | bytes 131088 | tf_op jit(solution)/shard_map/reduce_scatter | solution.py:80
  200.4 1.8 multiply_convert_fusion
  203.2 12.0 %copy.9 = bf16[1,1,256,128,128]{3,4,2,1,0:T(8,128)(2,1)} copy(bf16[1,1,256,128,128]{4,3,2,1,0:T(8,128)(2,1)} %bitcast.93) | data formatting | bytes 16777216 | tf_op args[3]
  216.4 27.5 %all-gather.2.cloned.1.call-done = bf16[4096,256]{1,0:T(8,128)(2,1)} async-done(((bf16[256,256]{1,0:T(8,128)(2,1)}), bf16[4096,256]{1,0:T(8,128)(2,1)}) %all-gather.2.cloned.1.call-update) | async-done | bytes 2097168 | tf_op jit(solution)/shard_map/all_gather | solution.py:89
  243.9 99.8 %while.23 = (s32[]{:T(128)}, f32[32,32768]{1,0:T(8,128)}, s32[4,64]{1,0:T(4,128)S(1)}, f32[4,64]{1,0:T(4,128)S(1)}, bf16[4,64,128,128]{2,3,1,0:T(8,128)(2,1)}, /...) while((s32[]{:T(128)}, f32[32,32768]{1,0:T(8,128)}, ...), condition=%wide.region_5.6_spmd.clone, body=%wide.region_4.5_spmd.clone.sunk | while | flops 1344279808 | bytes 56630384 | solution.py:45
  243.9 4.4 gather_fusion.1
  248.3 4.1 fusion.71
  252.4 8.0 %copy.17 = f32[8,8,128,256]{3,1,2,0:T(8,128)} copy(f32[8,8,128,256]{3,2,1,0:T(8,128)S(1)} %bitcast.89) | data formatting | bytes 16777216 | tf_op jit(solution)/shard_map/while
  260.3 8.0 %convolution_add_fusion.5 = f32[32,32768]{1,0:T(8,128)} fusion(f32[64,32768]{1,0:T(8,128)} %bitcast.87, f32[32,32768]{1,0:T(8,128)} %get-tuple-element.303, pred[]{:T(512)S(6)} %compare.7, f32[64]{0:T(128)S(1)} %fusion.72, s32[64]{0:T(128)S(1)} %fusion.73), kind=kOutput, calls=%fused_computation.24.clone.1 | convolution fusion | flops 807407616 | bytes 16777728 | tf_op jit(solution)/shard_map/while/body/eval_jaxpr/dot_general | solution.py:35
  268.3 4.4 gather_fusion.1
  272.7 4.1 fusion.71
  276.8 8.0 %copy.17 = f32[8,8,128,256]{3,1,2,0:T(8,128)} copy(f32[8,8,128,256]{3,2,1,0:T(8,128)S(1)} %bitcast.89) | data formatting | bytes 16777216 | tf_op jit(solution)/shard_map/while
  284.8 8.7 %convolution_add_fusion.5 = f32[32,32768]{1,0:T(8,128)} fusion(f32[64,32768]{1,0:T(8,128)} %bitcast.87, f32[32,32768]{1,0:T(8,128)} %get-tuple-element.303, pred[]{:T(512)S(6)} %compare.7, f32[64]{0:T(128)S(1)} %fusion.72, s32[64]{0:T(128)S(1)} %fusion.73), kind=kOutput, calls=%fused_computation.24.clone.1 | convolution fusion | flops 807407616 | bytes 16777728 | tf_op jit(solution)/shard_map/while/body/eval_jaxpr/dot_general | solution.py:35
  293.5 4.4 gather_fusion.1
  297.9 4.1 fusion.71
  301.9 8.0 %copy.17 = f32[8,8,128,256]{3,1,2,0:T(8,128)} copy(f32[8,8,128,256]{3,2,1,0:T(8,128)S(1)} %bitcast.89) | data formatting | bytes 16777216 | tf_op jit(solution)/shard_map/while
  309.9 8.6 %convolution_add_fusion.5 = f32[32,32768]{1,0:T(8,128)} fusion(f32[64,32768]{1,0:T(8,128)} %bitcast.87, f32[32,32768]{1,0:T(8,128)} %get-tuple-element.303, pred[]{:T(512)S(6)} %compare.7, f32[64]{0:T(128)S(1)} %fusion.72, s32[64]{0:T(128)S(1)} %fusion.73), kind=kOutput, calls=%fused_computation.24.clone.1 | convolution fusion | flops 807407616 | bytes 16777728 | tf_op jit(solution)/shard_map/while/body/eval_jaxpr/dot_general | solution.py:35
  318.6 4.4 gather_fusion.1
  323.0 4.1 fusion.71
  327.0 8.0 %copy.17 = f32[8,8,128,256]{3,1,2,0:T(8,128)} copy(f32[8,8,128,256]{3,2,1,0:T(8,128)S(1)} %bitcast.89) | data formatting | bytes 16777216 | tf_op jit(solution)/shard_map/while
  335.0 8.7 %convolution_add_fusion.5 = f32[32,32768]{1,0:T(8,128)} fusion(f32[64,32768]{1,0:T(8,128)} %bitcast.87, f32[32,32768]{1,0:T(8,128)} %get-tuple-element.303, pred[]{:T(512)S(6)} %compare.7, f32[64]{0:T(128)S(1)} %fusion.72, s32[64]{0:T(128)S(1)} %fusion.73), kind=kOutput, calls=%fused_computation.24.clone.1 | convolution fusion | flops 807407616 | bytes 16777728 | tf_op jit(solution)/shard_map/while/body/eval_jaxpr/dot_general | solution.py:35
  343.7 2.4 convert_element_type.38
  346.1 2.4 convert_element_type.39
  348.5 148.6 %all-reduce.2.cloned.1.call-done = f32[256,256]{1,0:T(8,128)} async-done(((f32[256,256]{1,0:T(8,128)}), f32[256,256]{1,0:T(8,128)}) %all-reduce.2.cloned.1.call-update) | async-done | bytes 262160 | tf_op jit(solution)/shard_map/psum | solution.py:93
  497.1 1.7 broadcast_multiply_fusion
  498.8 85.3 %reduce-scatter.5.cloned.1.call-done = bf16[256,256]{1,0:T(8,128)(2,1)} async-done(((bf16[4096,256]{1,0:T(8,128)(2,1)}), bf16[256,256]{1,0:T(8,128)(2,1)}) %reduce-scatter.5.cloned.1.call-update) | async-done | bytes 131088 | tf_op jit(solution)/shard_map/reduce_scatter | solution.py:95
  (58 shorter events, 2.6 us)
Async XLA Ops:
  7.2 193.2 %copy-start = (bf16[256,256]{1,0:T(8,128)(2,1)S(1)}, bf16[256,256]{1,0:T(8,128)(2,1)}, u32[]{:S(2)}) copy-start(bf16[256,256]{1,0:T(8,128)(2,1)} %param.11) | copy-start | bytes 393220
  7.2 9.6 %copy-start.3 = (s32[1,1,2,256]{3,2,1,0:T(2,128)S(1)}, s32[1,1,2,256]{3,2,1,0:T(2,128)}, u32[]{:S(2)}) copy-start(s32[1,1,2,256]{3,2,1,0:T(2,128)} %param.14) | copy-start | bytes 6148
  9.7 38.2 %all-to-all-start = ((bf16[16,256,256]{2,1,0:T(8,128)(2,1)}), bf16[16,256,256]{2,1,0:T(8,128)(2,1)S(1)}, u32[]{:S(2)}, u32[]{:S(2)}) async-start(bf16[16,256,256]{2,1,0:T(8,128)(2,1)} %stack.2), calls=%async_computation | async-start | bytes 4194304 | tf_op jit(solution)/shard_map/all_to_all | solution.py:68
  16.7 183.6 %reduce-scatter.3.cloned.1.call-start = ((), (), s32[]{:S(2)}) async-start(), calls=%async_computation.3 | async-start | bytes 2228224 | tf_op jit(solution)/shard_map/reduce_scatter | solution.py:80
  143.6 56.8 %copy-start.4 = (bf16[256,256]{1,0:T(8,128)(2,1)S(1)}, bf16[256,256]{1,0:T(8,128)(2,1)}, u32[]{:S(2)}) copy-start(bf16[256,256]{1,0:T(8,128)(2,1)} %param.12) | copy-start | bytes 393220
  146.0 98.0 %all-gather.2.cloned.1.call-start = ((), (), s32[]{:S(2)}) async-start(), calls=%async_computation.5 | async-start | bytes 2228224 | tf_op jit(solution)/shard_map/all_gather | solution.py:89
  203.1 12.1 %copy-start.2 = (bf16[256,256]{1,0:T(8,128)(2,1)S(1)}, bf16[256,256]{1,0:T(8,128)(2,1)}, u32[]{:S(2)}) copy-start(bf16[256,256]{1,0:T(8,128)(2,1)} %reduce-scatter.3.cloned.1.call-done) | copy-start | bytes 393220
  203.1 294.0 %all-reduce.2.cloned.1.call-start = ((), (), s32[]{:S(2)}) async-start(), calls=%async_computation.4 | async-start | bytes 524288 | tf_op jit(solution)/shard_map/psum | solution.py:93
  216.1 368.0 %reduce-scatter.5.cloned.1.call-start = ((), (), s32[]{:S(2)}) async-start(), calls=%async_computation.6 | async-start | bytes 2228224 | tf_op jit(solution)/shard_map/reduce_scatter | solution.py:95
  343.7 240.4 %copy-start.1 = (bf16[256,256]{1,0:T(8,128)(2,1)S(1)}, bf16[256,256]{1,0:T(8,128)(2,1)}, u32[]{:S(2)}) copy-start(bf16[256,256]{1,0:T(8,128)(2,1)} %param.11) | copy-start | bytes 393220
Sparse Core Ops, SparseCore 0:
  146.1 54.2 reduce-scatter.2
  203.2 40.6 all-gather.1
  249.9 247.1 all-reduce.1
  500.1 83.9 reduce-scatter.4
